TPU v7x, 32 devices: a whole 2x2x4 slice. The times are simulated.
32 devices in a mesh: parts: 2 (over x), owner: 4 (over y, core), helper: 4 (over z).
Axes of the slice: x: 2, y: 2, z: 4, core: 2. Of those that a mesh axis runs over, the one named last changes fastest.
Arguments:
- embeddings: bfloat16 [32768, 768], P(('parts', 'owner', 'helper')), parts along dimension 0
- cluster_sizes: int32 [64], P('parts'), parts along dimension 0, may hold values from 1 to 4096, 16384 in all
Outputs:
- nearest: float32 [32768], P(('parts', 'owner', 'helper')), parts along dimension 0
There are 2 independent parts, one for each index of `parts`. A program takes and returns all parts, laid end to end along the dimension named above; each array names one. Nothing has to cross between parts.
Inputs may be any that keep to these rules, and one draw needn't show every extreme that they name: `cluster_sizes`: the sizes add up to 16384; the largest is exactly 4096.
All inputs are finite; a program needn't handle non-finite values.
Results may differ from a plain program's by a relative error of at most 0.00053.
Values may be sent and summed in bfloat16 or wider, within the bound.
A program may use at most 64 MiB of HBM per device.

v0:
```python
import math

import jax
import jax.numpy as jnp
from jax import lax
from jax.sharding import PartitionSpec as P

REACH = 4


FLOOR = -2.0


def from_behind(value, axis, steps):
    count = lax.axis_size(axis)
    initial, last = (max(0, -steps), min(count, count - steps))
    return lax.ppermute(value, axis, [(source, source + steps) for source in range(initial, last)])


def normalize(embeddings):
    values = embeddings.astype(jnp.float32)
    factor = lax.rsqrt(jnp.mean(values * values, axis=1, keepdims=True) + 1e-06) * (
        1.0 / math.sqrt(values.shape[1])
    )
    return (values * factor).astype(jnp.bfloat16)


def cluster_of(first_row, row_total, cluster_ends):
    positions = first_row + jnp.arange(row_total, dtype=jnp.int32)
    located = jnp.sum((positions[:, None] >= cluster_ends[None, :]).astype(jnp.int32), axis=1)
    return jnp.where(positions < 0, -1, located)


def tile_best(row_unit, row_cluster, column_unit, column_cluster, skip_self):
    scores = lax.dot_general(
        row_unit, column_unit, (((1,), (1,)), ((), ())), preferred_element_type=jnp.float32
    )
    same_cluster = row_cluster[:, None] == column_cluster[None, :]
    if skip_self:
        row_total = row_unit.shape[0]
        same_cluster = same_cluster & (
            lax.broadcasted_iota(jnp.int32, (row_total, row_total), 0)
            != lax.broadcasted_iota(jnp.int32, (row_total, row_total), 1)
        )
    masked = jnp.where(same_cluster, scores, FLOOR)
    return (jnp.max(masked, axis=1), jnp.max(masked, axis=0))


def intersections(row_cluster, column_cluster):
    return (row_cluster[0] <= column_cluster[-1]) & (column_cluster[0] <= row_cluster[-1])


def body(embeddings, cluster_sizes):
    unit_rows = normalize(embeddings)
    row_total = unit_rows.shape[0]
    cluster_ends = jnp.cumsum(cluster_sizes)
    device_index = lax.axis_index(("owner", "helper"))
    first_row = device_index * row_total
    own_cluster = cluster_of(first_row, row_total, cluster_ends)
    best_score, unused = tile_best(unit_rows, own_cluster, unit_rows, own_cluster, True)
    blank = jnp.full((row_total,), FLOOR, jnp.float32)
    for offset in range(1, REACH + 1):
        lower_rows = from_behind(unit_rows, ("owner", "helper"), offset)
        lower_cluster = cluster_of(first_row - offset * row_total, row_total, cluster_ends)
        lower_best = lax.cond(
            intersections(own_cluster, lower_cluster),
            lambda: tile_best(unit_rows, own_cluster, lower_rows, lower_cluster, False)[0],
            lambda: blank,
        )
        best_score = jnp.maximum(best_score, lower_best)
        upper_rows = from_behind(unit_rows, ("owner", "helper"), -offset)
        upper_cluster = cluster_of(first_row + offset * row_total, row_total, cluster_ends)
        upper_best = lax.cond(
            intersections(own_cluster, upper_cluster),
            lambda: tile_best(unit_rows, own_cluster, upper_rows, upper_cluster, False)[0],
            lambda: blank,
        )
        best_score = jnp.maximum(best_score, upper_best)
    return jnp.maximum(best_score, -1.0)


def solution(mesh):
    placed = (P(("parts", "owner", "helper"), None), P("parts"))
    return jax.shard_map(
        body, mesh=mesh, in_specs=placed, out_specs=P(("parts", "owner", "helper")), check_vma=False
    )
```

profile of v0, /device:TPU:13, one launch (start us, length us, event | category | flops | bytes accessed | tf_op | source)
XLA Modules:
  0.0 284.3 jit_solution(4126871824964287449)
XLA Ops:
  0.0 0.0 copy-start
  0.0 1.9 fusion.1
  1.9 0.0 copy-done
  1.9 0.0 copy-start.1
  1.9 0.3 fusion.2
  2.3 4.2 %collective-permute-start.2 = (bf16[1024,768]{1,0:T(8,128)(2,1)S(1)}, bf16[1024,768]{1,0:T(8,128)(2,1)}, u32[]{:S(2)}, u32[]{:S(2)}) collective-permute-start(bf16[1024,768]{1,0:T(8,128)(2,1)S(1)} %fusion.2), channel_id=1, source_target_pairs={{0,2},{1,3},{2,4},{3,5},{4,6},{5,7},{6,8},{7,9},{8,10},{9,11},{10,... | collective-permute-start | bytes 4718600 | tf_op jit(solution)/shard_map/ppermute | solution.py:17
  6.5 2.5 collective-permute-start.3
  9.0 1.3 collective-permute-start.4
  10.3 5.6 %collective-permute-start.5 = (bf16[1024,768]{1,0:T(8,128)(2,1)S(1)}, bf16[1024,768]{1,0:T(8,128)(2,1)}, u32[]{:S(2)}, u32[]{:S(2)}) collective-permute-start(bf16[1024,768]{1,0:T(8,128)(2,1)S(1)} %fusion.2), channel_id=1, source_target_pairs={{3,0},{4,1},{5,2},{6,3},{7,4},{8,5},{9,6},{10,7},{11,8},{12,9},{13... | collective-permute-start | bytes 4718600 | tf_op jit(solution)/shard_map/ppermute | solution.py:17
  15.9 3.6 %collective-permute-start = (bf16[1024,768]{1,0:T(8,128)(2,1)S(1)}, bf16[1024,768]{1,0:T(8,128)(2,1)S(1)}, u32[]{:S(2)}, u32[]{:S(2)}) collective-permute-start(bf16[1024,768]{1,0:T(8,128)(2,1)S(1)} %fusion.2), channel_id=1, source_target_pairs={{0,1},{1,2},{2,3},{3,4},{4,5},{5,6},{6,7},{7,8},{8,9},{9,10},{10,1... | collective-permute-start | bytes 4718600 | tf_op jit(solution)/shard_map/ppermute | solution.py:17
  19.5 0.0 copy-done.1
  19.6 0.1 copy.5
  19.6 0.1 reduce-window.8
  19.7 0.1 reduce
  19.9 0.2 convert_reduce_fusion.7
  20.1 0.6 fusion.5
  20.8 0.6 fusion.10
  21.3 0.6 fusion.6
  22.0 0.6 fusion.7
  22.5 0.6 fusion.8
  23.2 118.5 %collective-permute-done.2 = bf16[1024,768]{1,0:T(8,128)(2,1)} collective-permute-done((bf16[1024,768]{1,0:T(8,128)(2,1)S(1)}, bf16[1024,768]{1,0:T(8,128)(2,1)}, u32[]{:S(2)}, u32[]{:S(2)}) %collective-permute-start.2) | collective-permute-done | bytes 1572896 | tf_op jit(solution)/shard_map/ppermute | solution.py:17
  141.6 2.5 collective-permute-start.1
  144.1 31.7 %collective-permute-done.3 = bf16[1024,768]{1,0:T(8,128)(2,1)} collective-permute-done((bf16[1024,768]{1,0:T(8,128)(2,1)S(1)}, bf16[1024,768]{1,0:T(8,128)(2,1)}, u32[]{:S(2)}, u32[]{:S(2)}) %collective-permute-start.3) | collective-permute-done | bytes 1572896 | tf_op jit(solution)/shard_map/ppermute | solution.py:17
  175.9 1.3 collective-permute-start.6
  177.1 15.9 %collective-permute-done.4 = bf16[1024,768]{1,0:T(8,128)(2,1)} collective-permute-done((bf16[1024,768]{1,0:T(8,128)(2,1)S(1)}, bf16[1024,768]{1,0:T(8,128)(2,1)}, u32[]{:S(2)}, u32[]{:S(2)}) %collective-permute-start.4) | collective-permute-done | bytes 1572896 | tf_op jit(solution)/shard_map/ppermute | solution.py:17
  193.1 54.6 %collective-permute-start.7 = (bf16[1024,768]{1,0:T(8,128)(2,1)S(1)}, bf16[1024,768]{1,0:T(8,128)(2,1)}, u32[]{:S(2)}, u32[]{:S(2)}) collective-permute-start(bf16[1024,768]{1,0:T(8,128)(2,1)S(1)} %fusion.2), channel_id=1, source_target_pairs={{4,0},{5,1},{6,2},{7,3},{8,4},{9,5},{10,6},{11,7},{12,8},{13,9},{1... | collective-permute-start | bytes 4718600 | tf_op jit(solution)/shard_map/ppermute | solution.py:17
  247.7 0.6 fusion.3
  260.5 0.6 fusion.4
  263.5 0.6 fusion.9
  266.5 0.6 fusion.11
  269.6 2.0 select_reduce_fusion.8
  271.6 3.3 %conditional.10 = (f32[1024]{0:T(1024)S(1)}) conditional(s32[]{:T(128)} %bitcast.3, () %tuple.57, (s32[1024]{0:T(1024)S(1)}, s32[1024]{0:T(1024)S(1)}, bf16[1024,768]{1,0:T(8,128)(2,1)S(1)}, bf16[1024,768]{1,0:T(8,128)(2,1)}) %tuple.58), branch_computations={%region_13.14_spmd, %region_14.16_spmd} | conditional | flops 1613757440 | bytes 3158024 | solution.py:65
  271.7 3.2 %select_reduce_fusion.2 = f32[1024]{0:T(1024)S(1)} fusion(s32[1024]{0:T(1024)S(1)} %get-tuple-element.101, s32[1024]{0:T(1024)S(1)} %get-tuple-element.102, bf16[1024,768]{1,0:T(8,128)(2,1)S(1)} %get-tuple-element.103, bf16[1024,768]{1,0:T(8,128)(2,1)} %get-tuple-element.104), kind=kOutput, calls=%fused_computation.2 | convolution fusion | flops 1613757440 | bytes 3158016 | tf_op jit(solution)/shard_map/cond/branch_1_fun/dot_general | solution.py:35
  274.9 3.3 %conditional.11 = (f32[1024]{0:T(1024)S(1)}) conditional(s32[]{:T(128)} %bitcast.4, () %tuple.59, (s32[1024]{0:T(1024)S(1)}, s32[1024]{0:T(1024)S(1)}, bf16[1024,768]{1,0:T(8,128)(2,1)S(1)}, bf16[1024,768]{1,0:T(8,128)(2,1)}) %tuple.60), branch_computations={%region_17.18_spmd, %region_18.20_spmd} | conditional | flops 1613757440 | bytes 3158024 | solution.py:73
  274.9 3.2 %select_reduce_fusion.3 = f32[1024]{0:T(1024)S(1)} fusion(s32[1024]{0:T(1024)S(1)} %get-tuple-element.105, s32[1024]{0:T(1024)S(1)} %get-tuple-element.106, bf16[1024,768]{1,0:T(8,128)(2,1)S(1)} %get-tuple-element.107, bf16[1024,768]{1,0:T(8,128)(2,1)} %get-tuple-element.108), kind=kOutput, calls=%fused_computation.3 | convolution fusion | flops 1613757440 | bytes 3158016 | tf_op jit(solution)/shard_map/cond/branch_1_fun/dot_general | solution.py:35
  278.2 0.0 collective-permute-done.5
  278.3 0.0 collective-permute-done
  278.3 1.9 conditional.8
  278.3 1.8 select_reduce_fusion
  280.1 0.0 collective-permute-done.1
  280.1 3.3 %conditional.9 = (f32[1024]{0:T(1024)S(1)}) conditional(s32[]{:T(128)} %bitcast.2, () %tuple.55, (s32[1024]{0:T(1024)S(1)}, s32[1024]{0:T(1024)S(1)}, bf16[1024,768]{1,0:T(8,128)(2,1)S(1)}, bf16[1024,768]{1,0:T(8,128)(2,1)}) %tuple.56), branch_computations={%region_9.10_spmd, %region_10.12_spmd} | conditional | flops 1613757440 | bytes 3158024 | solution.py:73
  280.2 3.2 %select_reduce_fusion.1 = f32[1024]{0:T(1024)S(1)} fusion(s32[1024]{0:T(1024)S(1)} %get-tuple-element.90, s32[1024]{0:T(1024)S(1)} %get-tuple-element.96, bf16[1024,768]{1,0:T(8,128)(2,1)S(1)} %get-tuple-element.98, bf16[1024,768]{1,0:T(8,128)(2,1)} %get-tuple-element.100), kind=kOutput, calls=%fused_computation.1 | convolution fusion | flops 1613757440 | bytes 3158016 | tf_op jit(solution)/shard_map/cond/branch_1_fun/dot_general | solution.py:35
  283.4 0.0 collective-permute-done.6
  283.4 0.2 conditional.14
  283.6 0.0 collective-permute-done.7
  283.7 0.6 maximum_maximum_fusion
  (22 shorter events, 0.2 us)
Async XLA Ops:
  0.0 1.9 copy-start
  1.9 17.6 %copy-start.1 = (s32[32]{0:T(128)S(1)}, s32[32]{0:T(128)}, u32[]{:S(2)}) copy-start(s32[32]{0:T(128)} %param.19) | copy-start | bytes 388
  2.3 139.4 %collective-permute-start.2 = (bf16[1024,768]{1,0:T(8,128)(2,1)S(1)}, bf16[1024,768]{1,0:T(8,128)(2,1)}, u32[]{:S(2)}, u32[]{:S(2)}) collective-permute-start(bf16[1024,768]{1,0:T(8,128)(2,1)S(1)} %fusion.2), channel_id=1, source_target_pairs={{0,2},{1,3},{2,4},{3,5},{4,6},{5,7},{6,8},{7,9},{8,10},{9,11},{10,... | collective-permute-start | bytes 4718600 | tf_op jit(solution)/shard_map/ppermute | solution.py:17
  6.5 169.4 %collective-permute-start.3 = (bf16[1024,768]{1,0:T(8,128)(2,1)S(1)}, bf16[1024,768]{1,0:T(8,128)(2,1)}, u32[]{:S(2)}, u32[]{:S(2)}) collective-permute-start(bf16[1024,768]{1,0:T(8,128)(2,1)S(1)} %fusion.2), channel_id=1, source_target_pairs={{2,0},{3,1},{4,2},{5,3},{6,4},{7,5},{8,6},{9,7},{10,8},{11,9},{12,... | collective-permute-start | bytes 4718600 | tf_op jit(solution)/shard_map/ppermute | solution.py:17
  9.0 184.1 %collective-permute-start.4 = (bf16[1024,768]{1,0:T(8,128)(2,1)S(1)}, bf16[1024,768]{1,0:T(8,128)(2,1)}, u32[]{:S(2)}, u32[]{:S(2)}) collective-permute-start(bf16[1024,768]{1,0:T(8,128)(2,1)S(1)} %fusion.2), channel_id=1, source_target_pairs={{0,3},{1,4},{2,5},{3,6},{4,7},{5,8},{6,9},{7,10},{8,11},{9,12},{10... | collective-permute-start | bytes 4718600 | tf_op jit(solution)/shard_map/ppermute | solution.py:17
  10.3 267.9 %collective-permute-start.5 = (bf16[1024,768]{1,0:T(8,128)(2,1)S(1)}, bf16[1024,768]{1,0:T(8,128)(2,1)}, u32[]{:S(2)}, u32[]{:S(2)}) collective-permute-start(bf16[1024,768]{1,0:T(8,128)(2,1)S(1)} %fusion.2), channel_id=1, source_target_pairs={{3,0},{4,1},{5,2},{6,3},{7,4},{8,5},{9,6},{10,7},{11,8},{12,9},{13... | collective-permute-start | bytes 4718600 | tf_op jit(solution)/shard_map/ppermute | solution.py:17
  15.9 262.4 %collective-permute-start = (bf16[1024,768]{1,0:T(8,128)(2,1)S(1)}, bf16[1024,768]{1,0:T(8,128)(2,1)S(1)}, u32[]{:S(2)}, u32[]{:S(2)}) collective-permute-start(bf16[1024,768]{1,0:T(8,128)(2,1)S(1)} %fusion.2), channel_id=1, source_target_pairs={{0,1},{1,2},{2,3},{3,4},{4,5},{5,6},{6,7},{7,8},{8,9},{9,10},{10,1... | collective-permute-start | bytes 4718600 | tf_op jit(solution)/shard_map/ppermute | solution.py:17
  141.6 138.5 %collective-permute-start.1 = (bf16[1024,768]{1,0:T(8,128)(2,1)S(1)}, bf16[1024,768]{1,0:T(8,128)(2,1)}, u32[]{:S(2)}, u32[]{:S(2)}) collective-permute-start(bf16[1024,768]{1,0:T(8,128)(2,1)S(1)} %fusion.2), channel_id=1, source_target_pairs={{1,0},{2,1},{3,2},{4,3},{5,4},{6,5},{7,6},{8,7},{9,8},{10,9},{11,1... | collective-permute-start | bytes 4718600 | tf_op jit(solution)/shard_map/ppermute | solution.py:17
  175.9 107.6 %collective-permute-start.6 = (bf16[1024,768]{1,0:T(8,128)(2,1)S(1)}, bf16[1024,768]{1,0:T(8,128)(2,1)}, u32[]{:S(2)}, u32[]{:S(2)}) collective-permute-start(bf16[1024,768]{1,0:T(8,128)(2,1)S(1)} %fusion.2), channel_id=1, source_target_pairs={{0,4},{1,5},{2,6},{3,7},{4,8},{5,9},{6,10},{7,11},{8,12},{9,13},{1... | collective-permute-start | bytes 4718600 | tf_op jit(solution)/shard_map/ppermute | solution.py:17
  193.1 90.6 %collective-permute-start.7 = (bf16[1024,768]{1,0:T(8,128)(2,1)S(1)}, bf16[1024,768]{1,0:T(8,128)(2,1)}, u32[]{:S(2)}, u32[]{:S(2)}) collective-permute-start(bf16[1024,768]{1,0:T(8,128)(2,1)S(1)} %fusion.2), channel_id=1, source_target_pairs={{4,0},{5,1},{6,2},{7,3},{8,4},{9,5},{10,6},{11,7},{12,8},{13,9},{1... | collective-permute-start | bytes 4718600 | tf_op jit(solution)/shard_map/ppermute | solution.py:17
where the time goes:
time: 285 us; the launch traced here: 284 us
  waiting for transfers between devices  166 us (58%)
  starting transfers between devices  75.6 us (27%)
  between operations  19.8 us (7%)
  matrix products  13.6 us (5%)
  local copies, waits for them, and re-layouts  5.52 us (2%)
  other arithmetic  3.34 us (1%)
    ppermute x8, waiting for transfers between devices, from_behind(): lax.ppermute(value, axis, [(source, source + steps) for source in range(i...  166 us
    ppermute x8, starting transfers between devices, from_behind(): lax.ppermute(value, axis, [(source, source + steps) for source in range(i...  75.6 us
    dot_general x5, matrix products, tile_best(): lax.dot_general(row_unit, column_unit, (((1,), (1,)), ((), ())), preferre...  13.6 us
  transfers between devices with their start and end apart: 8, of which 3 were waited for; matrix products, arithmetic and copies ran while one was open for 7% of the time, Pallas kernels for 0%

commit v1 on v0

--- a/solution.py
+++ b/solution.py
@@ -1,8 +1,11 @@
+import functools
 import math
 
 import jax
 import jax.numpy as jnp
 from jax import lax
+from jax.experimental import pallas as pl
+from jax.experimental.pallas import tpu as pltpu
 from jax.sharding import PartitionSpec as P
 
 REACH = 4
@@ -79,8 +82,320 @@
     return jnp.maximum(best_score, -1.0)
 
 
+CHUNK = 256
+MESH = pl.DeviceIdType.MESH
+
+
+def kernel(line, u_ref, slot_ids, own_ids, res_ids, part_ids, out_ref,
+           stream, part, row_best, res_best, part_best, own_best, message, returned, part_back,
+           own_send, own_recv, part_send, part_recv, flow_send, ret_send, ret_recv, pb_send, pb_recv):
+    rows = u_ref.shape[0]
+    chunks = rows // CHUNK
+    o, z = lax.axis_index("owner"), lax.axis_index("helper")
+    middle = ((o + 1) // 2) % 2
+    held = o + middle * (3 - 2 * o)
+    sibling = o + 1 - 2 * (o % 2)
+    ahead = 2 * (o % 2) - 1
+    is_middle = middle == 1
+
+    barrier = pltpu.get_barrier_semaphore()
+
+    def greet(owner, helper):
+        pl.semaphore_signal(barrier, inc=1, device_id={"owner": owner, "helper": helper}, device_id_type=MESH)
+
+    for step in range(1, line):
+        greet(o, lax.rem(z + step, line))
+    greet(sibling, z)
+
+    @pl.when(is_middle)
+    def _():
+        for helper in range(line):
+            greet(3 - o, jnp.int32(helper))
+        pl.semaphore_wait(barrier, 2 * line)
+
+    @pl.when(jnp.logical_not(is_middle))
+    def _():
+        pl.semaphore_wait(barrier, line)
+
+    def piece(c):
+        return pl.ds(pl.multiple_of(c * CHUNK, CHUNK), CHUNK)
+
+    def swap(c):
+        return pltpu.make_async_remote_copy(
+            src_ref=u_ref.at[piece(c)], dst_ref=stream.at[z, piece(c)],
+            send_sem=own_send.at[c], recv_sem=own_recv.at[z, c],
+            device_id={"owner": 3 - o, "helper": z}, device_id_type=MESH)
+
+    def keep(c):
+        return pltpu.make_async_copy(u_ref.at[piece(c)], stream.at[z, piece(c)], own_recv.at[z, c])
+
+    def flow(slot, c):
+        return pltpu.make_async_remote_copy(
+            src_ref=stream.at[slot, piece(c)], dst_ref=stream.at[slot, piece(c)],
+            send_sem=flow_send.at[slot, c], recv_sem=own_recv.at[slot, c],
+            device_id={"owner": o, "helper": z + ahead}, device_id_type=MESH)
+
+    partner = pltpu.make_async_remote_copy(
+        src_ref=u_ref, dst_ref=part, send_sem=part_send, recv_sem=part_recv,
+        device_id={"owner": sibling, "helper": z}, device_id_type=MESH)
+    partner_here = pltpu.make_async_copy(u_ref, part, part_recv)
+    has_next = (z + ahead >= 0) & (z + ahead < line)
+
+    @pl.when(is_middle)
+    def _():
+        for c in range(chunks):
+            swap(c).start()
+        partner.start()
+
+    @pl.when(jnp.logical_not(is_middle))
+    def _():
+        for c in range(chunks):
+            keep(c).start()
+
+    @pl.when(o == 2)
+    def _():
+        partner_here.start()
+
+    row_best[...] = jnp.full_like(row_best, FLOOR)
+    for ref in (res_best, part_best, own_best):
+        ref[...] = jnp.full_like(ref, FLOOR)
+
+    def columns_loop(block, ids, columns_ref, column_ids, best, row_total, diagonal):
+        def step(k, row_total):
+            at = pl.ds(pl.multiple_of(k * CHUNK, CHUNK), CHUNK)
+            scores = lax.dot_general(
+                block, columns_ref[at, :], (((1,), (1,)), ((), ())), preferred_element_type=jnp.float32)
+            same = ids == column_ids[:, at]
+            if diagonal is not None:
+                first = lax.broadcasted_iota(jnp.int32, scores.shape, 0) + diagonal * CHUNK
+                second = lax.broadcasted_iota(jnp.int32, scores.shape, 1) + k * CHUNK
+                same = same & (first != second)
+            scores = jnp.where(same, scores, FLOOR)
+            best[:, at] = jnp.maximum(best[:, at], jnp.max(scores.reshape(CHUNK // 8, 8, CHUNK), axis=0))
+            if row_total is None:
+                return None
+            return jnp.maximum(row_total, jnp.maximum(scores[:, :128], scores[:, 128:]))
+
+        return lax.fori_loop(0, rows // CHUNK, step, row_total)
+
+    def own_step(c, carry):
+        @pl.when(is_middle)
+        def _():
+            swap(c).wait_recv()
+
+        @pl.when(jnp.logical_not(is_middle))
+        def _():
+            keep(c).wait()
+
+        @pl.when(has_next)
+        def _():
+            flow(z, c).start()
+
+        return carry
+
+    def self_step(c, carry):
+        columns_loop(u_ref[piece(c), :], own_row(c), u_ref, own_ids, own_best, None, c)
+        return carry
+
+    def own_row(c):
+        return slot_ids[pl.ds(pl.multiple_of(line * rows + c * CHUNK, CHUNK), CHUNK), :]
+
+    def slot_row(slot, c):
+        return slot_ids[pl.ds(pl.multiple_of(slot * rows + c * CHUNK, CHUNK), CHUNK), :]
+
+    @pl.when(is_middle)
+    def _():
+        lax.fori_loop(0, chunks, self_step, 0)
+
+    lax.fori_loop(0, chunks, own_step, 0)
+
+    @pl.when(jnp.logical_not(is_middle))
+    def _():
+        lax.fori_loop(0, chunks, self_step, 0)
+        partner.wait_recv()
+
+    @pl.when(o == 2)
+    def _():
+        partner_here.wait()
+
+    def with_part(slot, c):
+        best = row_best.at[slot, piece(c)]
+        best[...] = columns_loop(stream[slot, piece(c), :], slot_row(slot, c), part, part_ids, part_best, best[...], None)
+
+    def part_step(c, carry):
+        with_part(z, c)
+        return carry
+
+    @pl.when(o != 1)
+    def _():
+        lax.fori_loop(0, chunks, part_step, 0)
+
+    def to_home(slot):
+        return pltpu.make_async_remote_copy(
+            src_ref=message.at[slot], dst_ref=returned.at[z],
+            send_sem=ret_send.at[slot], recv_sem=ret_recv.at[z],
+            device_id={"owner": held, "helper": slot}, device_id_type=MESH)
+
+    def from_holder(helper):
+        return pltpu.make_async_remote_copy(
+            src_ref=message.at[z], dst_ref=returned.at[helper],
+            send_sem=ret_send.at[z], recv_sem=ret_recv.at[helper],
+            device_id={"owner": held, "helper": helper}, device_id_type=MESH)
+
+    def folded(slot):
+        return jnp.max(row_best[slot].T.reshape(16, 8, rows), axis=0)
+
+    def flow_step(h, carry):
+        slot = z - h * ahead
+
+        @pl.when((slot >= 0) & (slot < line))
+        def _():
+            def chunk_step(c, carry):
+                flow(slot, c).wait_recv()
+
+                @pl.when(has_next)
+                def _():
+                    flow(slot, c).start()
+
+                best = row_best.at[slot, piece(c)]
+                best[...] = columns_loop(
+                    stream[slot, piece(c), :], slot_row(slot, c), stream.at[z], res_ids, res_best, best[...], None)
+
+                @pl.when(o != 1)
+                def _():
+                    with_part(slot, c)
+
+                return carry
+
+            lax.fori_loop(0, chunks, chunk_step, 0)
+            message[slot] = folded(slot)
+            to_home(slot).start()
+
+        return carry
+
+    lax.fori_loop(1, line, flow_step, 0)
+
+    message[z] = jnp.maximum(folded(z), res_best[...])
+    part_home = pltpu.make_async_remote_copy(
+        src_ref=part_best, dst_ref=part_back, send_sem=pb_send, recv_sem=pb_recv,
+        device_id={"owner": sibling, "helper": z}, device_id_type=MESH)
+
+    @pl.when(is_middle)
+    def _():
+        to_home(z).start()
+
+    @pl.when(jnp.logical_not(is_middle))
+    def _():
+        part_home.start()
+        own_best[...] = jnp.maximum(own_best[...], message[z])
+
+    @pl.when(o == 2)
+    def _():
+        own_best[...] = jnp.maximum(own_best[...], part_best[...])
+
+    @pl.when(is_middle)
+    def _():
+        from_holder(z).wait_recv()
+        own_best[...] = jnp.maximum(own_best[...], returned[z])
+        part_home.wait_recv()
+        own_best[...] = jnp.maximum(own_best[...], part_back[...])
+
+    back = 2 * (held % 2) - 1
+
+    def collect(h, carry):
+        helper = z + h * back
+
+        @pl.when((helper >= 0) & (helper < line))
+        def _():
+            from_holder(helper).wait_recv()
+            own_best[...] = jnp.maximum(own_best[...], returned[helper])
+
+        slot = z - h * ahead
+
+        @pl.when((slot >= 0) & (slot < line))
+        def _():
+            to_home(slot).wait_send()
+
+        return carry
+
+    lax.fori_loop(1, line, collect, 0)
+    out_ref[...] = jnp.maximum(jnp.max(own_best[...], axis=0, keepdims=True), -1.0)
+
+    @pl.when(is_middle)
+    def _():
+        to_home(z).wait_send()
+        for c in range(chunks):
+            swap(c).wait_send()
+        partner.wait_send()
+
+    @pl.when(jnp.logical_not(is_middle))
+    def _():
+        part_home.wait_send()
+
+    @pl.when(has_next)
+    def _():
+        def drain(h, carry):
+            slot = z - h * ahead
+
+            @pl.when((slot >= 0) & (slot < line))
+            def _():
+                for c in range(chunks):
+                    flow(slot, c).wait_send()
+
+            return carry
+
+        lax.fori_loop(0, line, drain, 0)
+
+
+def chain_body(line, embeddings, cluster_sizes):
+    unit_rows = normalize(embeddings)
+    rows, width = unit_rows.shape
+    ends = jnp.cumsum(cluster_sizes)
+    o, z = lax.axis_index("owner"), lax.axis_index("helper")
+    held = jnp.where((o == 1) | (o == 2), 3 - o, o)
+    ids = lambda block, total: cluster_of(block * rows, total, ends)
+    own_ids = ids(o * line + z, rows)
+    slot_ids = jnp.concatenate([ids(held * line, rows * line), own_ids])[:, None]
+    res_ids = ids(held * line + z, rows)[None]
+    part_ids = ids(jnp.where(o == 0, 1, 2) * line + z, rows)[None]
+    chunks = rows // CHUNK
+    best = pl.pallas_call(
+        functools.partial(kernel, line),
+        out_shape=jax.ShapeDtypeStruct((1, rows), jnp.float32),
+        in_specs=[pl.BlockSpec(memory_space=pltpu.VMEM)] * 5,
+        out_specs=pl.BlockSpec(memory_space=pltpu.VMEM),
+        scratch_shapes=[
+            pltpu.VMEM((line, rows, width), jnp.bfloat16),
+            pltpu.VMEM((rows, width), jnp.bfloat16),
+            pltpu.VMEM((line, rows, 128), jnp.float32),
+            pltpu.VMEM((8, rows), jnp.float32),
+            pltpu.VMEM((8, rows), jnp.float32),
+            pltpu.VMEM((8, rows), jnp.float32),
+            pltpu.VMEM((line, 8, rows), jnp.float32),
+            pltpu.VMEM((line, 8, rows), jnp.float32),
+            pltpu.VMEM((8, rows), jnp.float32),
+            pltpu.SemaphoreType.DMA((chunks,)),
+            pltpu.SemaphoreType.DMA((line, chunks)),
+            pltpu.SemaphoreType.DMA,
+            pltpu.SemaphoreType.DMA,
+            pltpu.SemaphoreType.DMA((line, chunks)),
+            pltpu.SemaphoreType.DMA((line,)),
+            pltpu.SemaphoreType.DMA((line,)),
+            pltpu.SemaphoreType.DMA,
+            pltpu.SemaphoreType.DMA,
+        ],
+        compiler_params=pltpu.CompilerParams(
+            collective_id=0, has_side_effects=True, vmem_limit_bytes=48 * 2**20
+        ),
+    )(unit_rows, slot_ids, own_ids[None], res_ids, part_ids)
+    return best.reshape(rows)
+
+
 def solution(mesh):
     placed = (P(("parts", "owner", "helper"), None), P("parts"))
+    line = mesh.shape["helper"]
+    chained = mesh.shape["owner"] == 4 and line == REACH
     return jax.shard_map(
-        body, mesh=mesh, in_specs=placed, out_specs=P(("parts", "owner", "helper")), check_vma=False
+        functools.partial(chain_body, line) if chained else body,
+        mesh=mesh, in_specs=placed, out_specs=P(("parts", "owner", "helper")), check_vma=False
     )

time: 285 us -> 77.6 us (0.27)
  the two profiles are of different devices: /device:TPU:13 before, /device:TPU:1 now
where the time goes in v1:
time: 77.6 us; the launch traced here: 77.5 us
  Pallas kernels  72.5 us (93%)
  other arithmetic  2.73 us (4%)
  local copies, waits for them, and re-layouts  2.12 us (3%)
    pallas_call x1, Pallas kernels, chain_body(): pl.pallas_call(functools.partial(kernel, line), out_shape=jax.ShapeDtypeS...  72.5 us
    reduce_sum x1, other arithmetic, normalize(): jnp.mean(values * values, axis=1, keepdims=True) + 1e-06  1.89 us

profile of v1, /device:TPU:1, one launch (start us, length us, event | category | flops | bytes accessed | tf_op | source)
XLA Modules:
  0.0 77.5 jit_solution(1193421087540497456)
XLA Ops:
  0.0 0.7 copy.6
  0.7 0.1 reduce-window.8
  0.8 0.1 reduce
  0.9 0.1 convert_reduce_fusion.1
  1.1 0.1 convert_reduce_fusion
  1.3 0.8 %copy.7.slot_ids = s32[5120,1]{1,0:T(8,128)S(1)} copy(s32[5120,1]{0,1:T(1,128)S(1)} %bitcast.7) | data formatting | bytes 40960 | tf_op jit(solution)/shard_map/broadcast_in_dim | solution.py:358
  2.0 0.0 copy-start
  2.1 1.9 %fusion = f32[1024]{0:T(1024)S(1)} fusion(bf16[1024,768]{1,0:T(8,128)(2,1)} %param.2), kind=kLoop, calls=%fused_computation.2 | loop fusion | flops 2358272 | bytes 1576960 | tf_op jit(solution)/shard_map/reduce_sum | solution.py:25
  4.0 0.0 copy-done
  4.0 0.3 fusion.1.u_ref
  4.4 72.5 %shard_map.28 = f32[1,1024]{1,0:T(1,128)S(1)} custom-call(bf16[1024,768]{1,0:T(8,128)(2,1)S(1)} %fusion.1.u_ref, s32[5120,1]{1,0:T(8,128)S(1)} %copy.7.slot_ids, s32[1,1024]{1,0:T(1,128)S(1)} %compare_select_fusion.2.own_ids, s32[1,1024]{1,0:T(1,128)S(1)} %compare_select_fusion.1.res_ids, s32[1,1024]{1,0:T(1,128)S(1)} %compare_select_fusion.part_ids), custom_call_target="tpu_custom_call" | custom-call | tf_op jit(solution)/shard_map/pallas_call | solution.py:362
  76.9 0.6 copy.9
  (10 shorter events, 0.1 us)
Async XLA Ops:
  2.0 2.0 %copy-start = (bf16[1024,768]{1,0:T(8,128)(2,1)S(1)}, bf16[1024,768]{1,0:T(8,128)(2,1)}, u32[]{:S(2)}) copy-start(bf16[1024,768]{1,0:T(8,128)(2,1)} %param.2) | copy-start | bytes 4718596

commit v2 on v0

--- a/solution.py
+++ b/solution.py
@@ -1,8 +1,11 @@
+import functools
 import math
 
 import jax
 import jax.numpy as jnp
 from jax import lax
+from jax.experimental import pallas as pl
+from jax.experimental.pallas import tpu as pltpu
 from jax.sharding import PartitionSpec as P
 
 REACH = 4
@@ -79,8 +82,397 @@
     return jnp.maximum(best_score, -1.0)
 
 
+CHUNK = 256
+MESH = pl.DeviceIdType.MESH
+
+
+def kernel(line, u_ref, slot_ids, own_ids, res_ids, part_ids, out_ref,
+           stream, part, row_best, res_best, part_best, own_best, message, returned, part_back, pair_back,
+           out_send, swap_send, own_recv, part_send, part_recv, flow_send, ret_send, ret_recv,
+           pb_send, pb_recv, pair_send, pair_recv):
+    rows = u_ref.shape[0]
+    chunks = rows // CHUNK
+    o, z = lax.axis_index("owner"), lax.axis_index("helper")
+    middle = ((o + 1) // 2) % 2
+    held = o + middle * (3 - 2 * o)
+    sibling = o + 1 - 2 * (o % 2)
+    near, outer = 1 + z // 2, 3 * (z // 2)
+    is_middle, is_end = middle == 1, middle == 0
+    is_inner, is_outer = z == near, z == outer
+    takes = near == 1 + o % 2
+    gives = near != 1 + o % 2
+
+    barrier = pltpu.get_barrier_semaphore()
+
+    def greet(owner, helper):
+        pl.semaphore_signal(barrier, inc=1, device_id={"owner": owner, "helper": helper}, device_id_type=MESH)
+
+    for step in range(1, line):
+        greet(o, lax.rem(z + step, line))
+    for helper in range(line):
+        greet(sibling, jnp.int32(helper))
+
+    @pl.when(is_middle)
+    def _():
+        for helper in range(line):
+            greet(3 - o, jnp.int32(helper))
+        pl.semaphore_wait(barrier, 3 * line - 1)
+
+    @pl.when(is_end)
+    def _():
+        pl.semaphore_wait(barrier, 2 * line - 1)
+
+    def piece(c):
+        return pl.ds(pl.multiple_of(c * CHUNK, CHUNK), CHUNK)
+
+    def remote(src, dst, send, recv, owner, helper):
+        return pltpu.make_async_remote_copy(
+            src_ref=src, dst_ref=dst, send_sem=send, recv_sem=recv,
+            device_id={"owner": owner, "helper": helper}, device_id_type=MESH)
+
+    def inward_end(c):
+        return remote(u_ref.at[piece(c)], stream.at[outer, piece(c)], out_send.at[c], own_recv.at[outer, c], o, near)
+
+    def inward_middle(c):
+        return remote(u_ref.at[piece(c)], part.at[1, piece(c)], out_send.at[c], part_recv.at[1, c], o, near)
+
+    def swap_near(c):
+        return remote(u_ref.at[piece(c)], stream.at[near, piece(c)], swap_send.at[0, c], own_recv.at[near, c], 3 - o, near)
+
+    def swap_outer(c):
+        return remote(part.at[1, piece(c)], stream.at[outer, piece(c)], swap_send.at[1, c], own_recv.at[outer, c], 3 - o, near)
+
+    def share_near(c):
+        return remote(u_ref.at[piece(c)], part.at[0, piece(c)], part_send.at[0, c], part_recv.at[0, c], sibling, near)
+
+    def share_outer(c):
+        return remote(part.at[1, piece(c)], part.at[1, piece(c)], part_send.at[1, c], part_recv.at[1, c], sibling, near)
+
+    def keep(c):
+        return pltpu.make_async_copy(u_ref.at[piece(c)], stream.at[near, piece(c)], own_recv.at[near, c])
+
+    def keep_part(c):
+        return pltpu.make_async_copy(u_ref.at[piece(c)], part.at[0, piece(c)], part_recv.at[0, c])
+
+    def flow(slot, c):
+        return remote(stream.at[slot, piece(c)], stream.at[slot, piece(c)], flow_send.at[slot, c], own_recv.at[slot, c], o, 3 - near)
+
+    def each_chunk(action):
+        def step(c, carry):
+            action(c)
+            return carry
+
+        lax.fori_loop(0, chunks, step, 0)
+
+    def columns_loop(block, ids, columns_ref, column_ids, best, row_total, diagonal):
+        def step(k, row_total):
+            at = pl.ds(pl.multiple_of(k * CHUNK, CHUNK), CHUNK)
+            scores = lax.dot_general(
+                block, columns_ref[at, :], (((1,), (1,)), ((), ())), preferred_element_type=jnp.float32)
+            same = ids == column_ids[:, at]
+            if diagonal is not None:
+                first = lax.broadcasted_iota(jnp.int32, scores.shape, 0) + diagonal * CHUNK
+                second = lax.broadcasted_iota(jnp.int32, scores.shape, 1) + k * CHUNK
+                same = same & (first != second)
+            scores = jnp.where(same, scores, FLOOR)
+            best[:, at] = jnp.maximum(best[:, at], jnp.max(scores.reshape(CHUNK // 8, 8, CHUNK), axis=0))
+            if row_total is None:
+                return None
+            return jnp.maximum(row_total, jnp.maximum(scores[:, :128], scores[:, 128:]))
+
+        return lax.fori_loop(0, rows // CHUNK, step, row_total)
+
+    def slot_row(slot, c):
+        return slot_ids[pl.ds(pl.multiple_of(slot * rows + c * CHUNK, CHUNK), CHUNK), :]
+
+    def self_chunk(c):
+        columns_loop(u_ref[piece(c), :], slot_row(line, c), u_ref, own_ids, own_best, None, c)
+
+    def with_res(slot, c, which):
+        best = row_best.at[slot, piece(c)]
+        best[...] = columns_loop(
+            stream[slot, piece(c), :], slot_row(slot, c), stream.at[near if which == 0 else outer],
+            res_ids.at[which:which + 1], res_best.at[which], best[...], None)
+
+    def with_part(slot, c, which):
+        best = row_best.at[slot, piece(c)]
+        best[...] = columns_loop(
+            stream[slot, piece(c), :], slot_row(slot, c), part.at[which],
+            part_ids.at[which:which + 1], part_best.at[which], best[...], None)
+
+    def folded(slot):
+        return jnp.max(row_best[slot].T.reshape(16, 8, rows), axis=0)
+
+    def to_home(slot):
+        return remote(message.at[slot], returned.at[near - 1], ret_send.at[slot], ret_recv.at[near - 1], held, slot)
+
+    def from_holder(which):
+        return remote(message.at[z], returned.at[which], ret_send.at[z], ret_recv.at[which], held, near)
+
+    def part_home(which):
+        return remote(part_best.at[which], part_back, pb_send.at[which], pb_recv, sibling, near if which == 0 else outer)
+
+    pair_home = remote(part_best.at[1], pair_back, pair_send, pair_recv, o, outer)
+    there, there_outer = 3 - near, 3 - outer
+
+    own_best[...] = jnp.full_like(own_best, FLOOR)
+
+    @pl.when(is_outer)
+    def _():
+        @pl.when(is_end)
+        def _():
+            each_chunk(lambda c: inward_end(c).start())
+
+        @pl.when(is_middle)
+        def _():
+            each_chunk(lambda c: inward_middle(c).start())
+
+        each_chunk(self_chunk)
+
+    @pl.when(is_inner)
+    def _():
+        @pl.when(is_middle)
+        def _():
+            each_chunk(lambda c: swap_near(c).start())
+            each_chunk(lambda c: share_near(c).start())
+
+        @pl.when(is_end)
+        def _():
+            each_chunk(lambda c: keep(c).start())
+
+        @pl.when(o == 2)
+        def _():
+            each_chunk(lambda c: keep_part(c).start())
+
+        row_best[...] = jnp.full_like(row_best, FLOOR)
+        res_best[...] = jnp.full_like(res_best, FLOOR)
+        part_best[...] = jnp.full_like(part_best, FLOOR)
+
+        def first(c):
+            @pl.when(is_middle)
+            def _():
+                swap_near(c).wait_recv()
+
+            @pl.when(is_end)
+            def _():
+                keep(c).wait()
+
+            @pl.when(gives)
+            def _():
+                flow(near, c).start()
+
+            @pl.when(is_middle)
+            def _():
+                inward_middle(c).wait_recv()
+                swap_outer(c).start()
+                share_outer(c).start()
+
+            @pl.when(is_end)
+            def _():
+                inward_end(c).wait_recv()
+
+                @pl.when(gives)
+                def _():
+                    flow(outer, c).start()
+
+            self_chunk(c)
+
+        each_chunk(first)
+
+        def second(c):
+            @pl.when(is_middle)
+            def _():
+                swap_outer(c).wait_recv()
+
+                @pl.when(gives)
+                def _():
+                    flow(outer, c).start()
+
+            with_res(outer, c, 0)
+
+            @pl.when(takes)
+            def _():
+                flow(there, c).wait_recv()
+                with_res(there, c, 0)
+
+        each_chunk(second)
+
+        @pl.when(is_end)
+        def _():
+            each_chunk(lambda c: share_near(c).wait_recv())
+            each_chunk(lambda c: share_outer(c).wait_recv())
+
+        @pl.when(o == 2)
+        def _():
+            each_chunk(lambda c: keep_part(c).wait())
+
+        def third(c):
+            @pl.when(o != 1)
+            def _():
+                for which in range(2):
+                    with_part(near, c, which)
+                    with_part(outer, c, which)
+
+            @pl.when(takes)
+            def _():
+                with_res(there, c, 1)
+
+                @pl.when(o != 1)
+                def _():
+                    for which in range(2):
+                        with_part(there, c, which)
+
+        each_chunk(third)
+
+        @pl.when(takes)
+        def _():
+            message[there] = folded(there)
+            to_home(there).start()
+
+            def fourth(c):
+                flow(there_outer, c).wait_recv()
+                for which in range(2):
+                    with_res(there_outer, c, which)
+
+                @pl.when(o != 1)
+                def _():
+                    for which in range(2):
+                        with_part(there_outer, c, which)
+
+            each_chunk(fourth)
+            message[there_outer] = folded(there_outer)
+            to_home(there_outer).start()
+
+        message[outer] = jnp.maximum(folded(outer), res_best[1])
+        to_home(outer).start()
+        message[near] = jnp.maximum(folded(near), res_best[0])
+
+        @pl.when(is_middle)
+        def _():
+            to_home(near).start()
+
+        @pl.when(is_end)
+        def _():
+            part_home(0).start()
+            part_home(1).start()
+            own_best[...] = jnp.maximum(own_best[...], message[near])
+
+        @pl.when(o == 2)
+        def _():
+            pair_home.start()
+            own_best[...] = jnp.maximum(own_best[...], part_best[0])
+
+    @pl.when(is_outer | is_middle)
+    def _():
+        from_holder(near - 1).wait_recv()
+        own_best[...] = jnp.maximum(own_best[...], returned[near - 1])
+
+    @pl.when(near != 1 + held % 2)
+    def _():
+        from_holder(2 - near).wait_recv()
+        own_best[...] = jnp.maximum(own_best[...], returned[2 - near])
+
+    @pl.when(is_middle)
+    def _():
+        part_home(0).wait_recv()
+        own_best[...] = jnp.maximum(own_best[...], part_back[...])
+
+    @pl.when((o == 2) & is_outer)
+    def _():
+        pair_home.wait_recv()
+        own_best[...] = jnp.maximum(own_best[...], pair_back[...])
+
+    out_ref[...] = jnp.maximum(jnp.max(own_best[...], axis=0, keepdims=True), -1.0)
+
+    @pl.when(is_outer)
+    def _():
+        each_chunk(lambda c: inward_end(c).wait_send())
+
+    @pl.when(is_inner)
+    def _():
+        to_home(outer).wait_send()
+
+        @pl.when(takes)
+        def _():
+            to_home(there).wait_send()
+            to_home(there_outer).wait_send()
+
+        @pl.when(gives)
+        def _():
+            each_chunk(lambda c: flow(near, c).wait_send())
+            each_chunk(lambda c: flow(outer, c).wait_send())
+
+        @pl.when(is_middle)
+        def _():
+            to_home(near).wait_send()
+            for copy in (swap_near, swap_outer, share_near, share_outer):
+                each_chunk(lambda c, copy=copy: copy(c).wait_send())
+
+        @pl.when(is_end)
+        def _():
+            part_home(0).wait_send()
+            part_home(1).wait_send()
+
+        @pl.when(o == 2)
+        def _():
+            pair_home.wait_send()
+
+
+def chain_body(line, embeddings, cluster_sizes):
+    unit_rows = normalize(embeddings)
+    rows, width = unit_rows.shape
+    ends = jnp.cumsum(cluster_sizes)
+    o, z = lax.axis_index("owner"), lax.axis_index("helper")
+    held = jnp.where((o == 1) | (o == 2), 3 - o, o)
+    ids = lambda block, total: cluster_of(block * rows, total, ends)
+    own_ids = ids(o * line + z, rows)
+    slot_ids = jnp.concatenate([ids(held * line, rows * line), own_ids])[:, None]
+    near, outer = 1 + z // 2, 3 * (z // 2)
+    shared = jnp.where(o == 0, 1, 2) * line
+    res_ids = jnp.stack([ids(held * line + near, rows), ids(held * line + outer, rows)])
+    part_ids = jnp.stack([ids(shared + near, rows), ids(shared + outer, rows)])
+    chunks = rows // CHUNK
+    best = pl.pallas_call(
+        functools.partial(kernel, line),
+        out_shape=jax.ShapeDtypeStruct((1, rows), jnp.float32),
+        in_specs=[pl.BlockSpec(memory_space=pltpu.VMEM)] * 5,
+        out_specs=pl.BlockSpec(memory_space=pltpu.VMEM),
+        scratch_shapes=[
+            pltpu.VMEM((line, rows, width), jnp.bfloat16),
+            pltpu.VMEM((2, rows, width), jnp.bfloat16),
+            pltpu.VMEM((line, rows, 128), jnp.float32),
+            pltpu.VMEM((2, 8, rows), jnp.float32),
+            pltpu.VMEM((2, 8, rows), jnp.float32),
+            pltpu.VMEM((8, rows), jnp.float32),
+            pltpu.VMEM((line, 8, rows), jnp.float32),
+            pltpu.VMEM((2, 8, rows), jnp.float32),
+            pltpu.VMEM((8, rows), jnp.float32),
+            pltpu.VMEM((8, rows), jnp.float32),
+            pltpu.SemaphoreType.DMA((chunks,)),
+            pltpu.SemaphoreType.DMA((2, chunks)),
+            pltpu.SemaphoreType.DMA((line, chunks)),
+            pltpu.SemaphoreType.DMA((2, chunks)),
+            pltpu.SemaphoreType.DMA((2, chunks)),
+            pltpu.SemaphoreType.DMA((line, chunks)),
+            pltpu.SemaphoreType.DMA((line,)),
+            pltpu.SemaphoreType.DMA((2,)),
+            pltpu.SemaphoreType.DMA((2,)),
+            pltpu.SemaphoreType.DMA,
+            pltpu.SemaphoreType.DMA,
+            pltpu.SemaphoreType.DMA,
+        ],
+        compiler_params=pltpu.CompilerParams(
+            collective_id=0, has_side_effects=True, vmem_limit_bytes=48 * 2**20
+        ),
+    )(unit_rows, slot_ids, own_ids[None], res_ids, part_ids)
+    return best.reshape(rows)
+
+
 def solution(mesh):
     placed = (P(("parts", "owner", "helper"), None), P("parts"))
+    line = mesh.shape["helper"]
+    chained = mesh.shape["owner"] == 4 and line == REACH
     return jax.shard_map(
-        body, mesh=mesh, in_specs=placed, out_specs=P(("parts", "owner", "helper")), check_vma=False
+        functools.partial(chain_body, line) if chained else body,
+        mesh=mesh, in_specs=placed, out_specs=P(("parts", "owner", "helper")), check_vma=False
     )

time: 285 us -> 120 us (0.42)
  the two profiles are of different devices: /device:TPU:13 before, /device:TPU:1 now
where the time goes in v2:
time: 120 us; the launch traced here: 119 us
  Pallas kernels  114 us (95%)
  other arithmetic  2.81 us (2%)
  local copies, waits for them, and re-layouts  2.12 us (2%)
    pallas_call x1, Pallas kernels, chain_body(): pl.pallas_call(functools.partial(kernel, line), out_shape=jax.ShapeDtypeS...  114 us

profile of v2, /device:TPU:1, one launch (start us, length us, event | category | flops | bytes accessed | tf_op | source)
XLA Modules:
  0.0 119.4 jit_solution(4027978158839803206)
XLA Ops:
  0.0 0.7 copy.6
  0.8 0.1 reduce-window.8
  0.8 0.1 reduce
  0.9 0.2 convert_reduce_fusion.2
  1.1 0.1 convert_reduce_fusion
  1.3 0.8 copy.7.slot_ids
  2.1 0.0 copy-start
  2.3 1.9 %fusion = f32[1024]{0:T(1024)S(1)} fusion(bf16[1024,768]{1,0:T(8,128)(2,1)} %param.2), kind=kLoop, calls=%fused_computation.2 | loop fusion | flops 2358272 | bytes 1576960 | tf_op jit(solution)/shard_map/reduce_sum | solution.py:25
  4.2 0.0 copy-done
  4.2 0.3 fusion.1.u_ref
  4.5 114.3 %shard_map.28 = f32[1,1024]{1,0:T(1,128)S(1)} custom-call(bf16[1024,768]{1,0:T(8,128)(2,1)S(1)} %fusion.1.u_ref, s32[5120,1]{1,0:T(8,128)S(1)} %copy.7.slot_ids, s32[1,1024]{1,0:T(1,128)S(1)} %compare_select_fusion.4.own_ids, s32[2,1024]{1,0:T(2,128)S(1)} %pad_add_fusion.1.res_ids, s32[2,1024]{1,0:T(2,128)S(1)} %pad_add_fusion.2.part_ids), custom_call_target="tpu_custom_call" | custom-call | tf_op jit(solution)/shard_map/pallas_call | solution.py:435
  118.8 0.6 copy.9
  (15 shorter events, 0.1 us)
Async XLA Ops:
  2.1 2.0 %copy-start = (bf16[1024,768]{1,0:T(8,128)(2,1)S(1)}, bf16[1024,768]{1,0:T(8,128)(2,1)}, u32[]{:S(2)}) copy-start(bf16[1024,768]{1,0:T(8,128)(2,1)} %param.2) | copy-start | bytes 4718596

commit v3 on v2

--- a/solution.py
+++ b/solution.py
@@ -83,13 +83,14 @@
 
 
 CHUNK = 256
+GROUP = 2
 MESH = pl.DeviceIdType.MESH
 
 
 def kernel(line, u_ref, slot_ids, own_ids, res_ids, part_ids, out_ref,
            stream, part, row_best, res_best, part_best, own_best, message, returned, part_back, pair_back,
            out_send, swap_send, own_recv, part_send, part_recv, flow_send, ret_send, ret_recv,
-           pb_send, pb_recv, pair_send, pair_recv):
+           pb_send, pb_recv, pair_send, pair_recv, turn):
     rows = u_ref.shape[0]
     chunks = rows // CHUNK
     o, z = lax.axis_index("owner"), lax.axis_index("helper")
@@ -175,29 +176,43 @@
                 second = lax.broadcasted_iota(jnp.int32, scores.shape, 1) + k * CHUNK
                 same = same & (first != second)
             scores = jnp.where(same, scores, FLOOR)
-            best[:, at] = jnp.maximum(best[:, at], jnp.max(scores.reshape(CHUNK // 8, 8, CHUNK), axis=0))
+            best[:, at] = jnp.maximum(best[:, at], jnp.max(scores.reshape(-1, 8, CHUNK), axis=0))
             if row_total is None:
                 return None
             return jnp.maximum(row_total, jnp.maximum(scores[:, :128], scores[:, 128:]))
 
-        return lax.fori_loop(0, rows // CHUNK, step, row_total)
-
-    def slot_row(slot, c):
-        return slot_ids[pl.ds(pl.multiple_of(slot * rows + c * CHUNK, CHUNK), CHUNK), :]
+        return lax.fori_loop(0, rows // CHUNK, step, row_total, unroll=True)
+
+    def slot_row(slot, c, size=CHUNK):
+        return slot_ids[pl.ds(pl.multiple_of(slot * rows + c * size, size), size), :]
+
+    def group(g):
+        return pl.ds(pl.multiple_of(g * GROUP * CHUNK, GROUP * CHUNK), GROUP * CHUNK)
+
+    def each_group(action):
+        def step(g, carry):
+            action(g)
+            return carry
+
+        lax.fori_loop(0, chunks // GROUP, step, 0)
+
+    def in_group(g, action):
+        for i in range(GROUP):
+            action(g * GROUP + i)
 
     def self_chunk(c):
         columns_loop(u_ref[piece(c), :], slot_row(line, c), u_ref, own_ids, own_best, None, c)
 
-    def with_res(slot, c, which):
-        best = row_best.at[slot, piece(c)]
+    def with_res(slot, g, which):
+        best = row_best.at[slot, group(g)]
         best[...] = columns_loop(
-            stream[slot, piece(c), :], slot_row(slot, c), stream.at[near if which == 0 else outer],
+            stream[slot, group(g), :], slot_row(slot, g, GROUP * CHUNK), stream.at[near if which == 0 else outer],
             res_ids.at[which:which + 1], res_best.at[which], best[...], None)
 
-    def with_part(slot, c, which):
-        best = row_best.at[slot, piece(c)]
+    def with_part(slot, g, which):
+        best = row_best.at[slot, group(g)]
         best[...] = columns_loop(
-            stream[slot, piece(c), :], slot_row(slot, c), part.at[which],
+            stream[slot, group(g), :], slot_row(slot, g, GROUP * CHUNK), part.at[which],
             part_ids.at[which:which + 1], part_best.at[which], best[...], None)
 
     def folded(slot):
@@ -219,13 +234,18 @@
 
     @pl.when(is_outer)
     def _():
-        @pl.when(is_end)
-        def _():
+        @pl.when(is_middle)
+        def _():
+            each_chunk(lambda c: inward_middle(c).start())
+            for c in range(chunks - 1):
+                inward_middle(c).wait_send()
+            pl.semaphore_signal(turn, inc=1, device_id={"owner": sibling, "helper": outer}, device_id_type=MESH)
+            inward_middle(chunks - 1).wait_send()
+
+        @pl.when(is_end)
+        def _():
+            pl.semaphore_wait(turn, 1)
             each_chunk(lambda c: inward_end(c).start())
-
-        @pl.when(is_middle)
-        def _():
-            each_chunk(lambda c: inward_middle(c).start())
 
         each_chunk(self_chunk)
 
@@ -248,98 +268,109 @@
         res_best[...] = jnp.full_like(res_best, FLOOR)
         part_best[...] = jnp.full_like(part_best, FLOOR)
 
-        def first(c):
-            @pl.when(is_middle)
-            def _():
-                swap_near(c).wait_recv()
-
-            @pl.when(is_end)
-            def _():
-                keep(c).wait()
+        def kept(c):
+            keep(c).wait()
 
             @pl.when(gives)
             def _():
                 flow(near, c).start()
 
+        @pl.when(is_end)
+        def _():
+            each_chunk(kept)
+
+            each_chunk(self_chunk)
+
+        def first(c):
+            swap_near(c).wait_recv()
+
+            @pl.when(gives)
+            def _():
+                flow(near, c).start()
+
+            inward_middle(c).wait_recv()
+            swap_outer(c).start()
+            share_outer(c).start()
+            self_chunk(c)
+
+        @pl.when(is_middle)
+        def _():
+            each_chunk(first)
+
+        @pl.when(is_end)
+        def _():
+            each_chunk(lambda c: share_near(c).wait_recv())
+
+        @pl.when(o == 2)
+        def _():
+            each_chunk(lambda c: keep_part(c).wait())
+
+        @pl.when(o != 1)
+        def _():
+            each_group(lambda g: with_part(near, g, 0))
+
+        @pl.when(is_end)
+        def _():
+            each_chunk(lambda c: share_outer(c).wait_recv())
+
+        @pl.when(takes)
+        def _():
+            def early(g):
+                in_group(g, lambda c: flow(there, c).wait_recv())
+                with_res(there, g, 0)
+
+                @pl.when(o != 1)
+                def _():
+                    with_part(near, g, 1)
+                    for which in range(2):
+                        with_part(there, g, which)
+
+            each_group(early)
+
+        def relay(c):
             @pl.when(is_middle)
             def _():
-                inward_middle(c).wait_recv()
-                swap_outer(c).start()
-                share_outer(c).start()
+                swap_outer(c).wait_recv()
 
             @pl.when(is_end)
             def _():
                 inward_end(c).wait_recv()
 
+            @pl.when(gives)
+            def _():
+                flow(outer, c).start()
+
+        def late(g):
+            in_group(g, relay)
+            with_res(outer, g, 0)
+
+            @pl.when(o != 1)
+            def _():
+                with_part(outer, g, 1)
+
                 @pl.when(gives)
                 def _():
-                    flow(outer, c).start()
-
-            self_chunk(c)
-
-        each_chunk(first)
-
-        def second(c):
-            @pl.when(is_middle)
-            def _():
-                swap_outer(c).wait_recv()
-
-                @pl.when(gives)
-                def _():
-                    flow(outer, c).start()
-
-            with_res(outer, c, 0)
-
-            @pl.when(takes)
-            def _():
-                flow(there, c).wait_recv()
-                with_res(there, c, 0)
-
-        each_chunk(second)
-
-        @pl.when(is_end)
-        def _():
-            each_chunk(lambda c: share_near(c).wait_recv())
-            each_chunk(lambda c: share_outer(c).wait_recv())
-
-        @pl.when(o == 2)
-        def _():
-            each_chunk(lambda c: keep_part(c).wait())
-
-        def third(c):
-            @pl.when(o != 1)
-            def _():
+                    with_part(outer, g, 0)
+
+        each_group(late)
+
+        @pl.when(takes)
+        def _():
+            each_group(lambda g: with_res(there, g, 1))
+            message[there] = folded(there)
+            to_home(there).start()
+
+            def last(g):
+                in_group(g, lambda c: flow(there_outer, c).wait_recv())
                 for which in range(2):
-                    with_part(near, c, which)
-                    with_part(outer, c, which)
-
-            @pl.when(takes)
-            def _():
-                with_res(there, c, 1)
+                    with_res(there_outer, g, which)
 
                 @pl.when(o != 1)
                 def _():
                     for which in range(2):
-                        with_part(there, c, which)
-
-        each_chunk(third)
-
-        @pl.when(takes)
-        def _():
-            message[there] = folded(there)
-            to_home(there).start()
-
-            def fourth(c):
-                flow(there_outer, c).wait_recv()
-                for which in range(2):
-                    with_res(there_outer, c, which)
-
-                @pl.when(o != 1)
-                def _():
-                    for which in range(2):
-                        with_part(there_outer, c, which)
-
-            each_chunk(fourth)
+                        with_part(there_outer, g, which)
+
+            each_group(last)
             message[there_outer] = folded(there_outer)
             to_home(there_outer).start()
 
@@ -384,7 +415,7 @@
 
     out_ref[...] = jnp.maximum(jnp.max(own_best[...], axis=0, keepdims=True), -1.0)
 
-    @pl.when(is_outer)
+    @pl.when(is_outer & is_end)
     def _():
         each_chunk(lambda c: inward_end(c).wait_send())
 
@@ -460,6 +491,7 @@
             pltpu.SemaphoreType.DMA,
             pltpu.SemaphoreType.DMA,
             pltpu.SemaphoreType.DMA,
+            pltpu.SemaphoreType.REGULAR,
         ],
         compiler_params=pltpu.CompilerParams(
             collective_id=0, has_side_effects=True, vmem_limit_bytes=48 * 2**20

time: 120 us -> 62.8 us (0.52)
  Pallas kernels: 114 us -> 57.3 us
    pallas_call x1, Pallas kernels: 114 us -> 57.3 us  [chain_body(): pl.pallas_call(functools.partial(kernel, line), out_shape=jax.ShapeDtypeS...]
where the time goes in v3:
time: 62.8 us; the launch traced here: 62.4 us
  Pallas kernels  57.3 us (91%)
  other arithmetic  2.81 us (4%)
  local copies, waits for them, and re-layouts  2.12 us (3%)
    pallas_call x1, Pallas kernels, chain_body(): pl.pallas_call(functools.partial(kernel, line), out_shape=jax.ShapeDtypeS...  57.3 us
    reduce_sum x1, other arithmetic, normalize(): jnp.mean(values * values, axis=1, keepdims=True) + 1e-06  1.88 us

profile of v3, /device:TPU:1, one launch (start us, length us, event | category | flops | bytes accessed | tf_op | source)
XLA Modules:
  0.0 62.4 jit_solution(12852106653435852616)
XLA Ops:
  0.0 0.7 %copy.6 = s32[32,1]{1,0:T(8,128)S(1)} copy(s32[32,1]{0,1:T(1,128)} %bitcast.15) | data formatting | bytes 256 | tf_op jit(solution)/shard_map/reshape.136
  0.8 0.1 reduce-window.8
  0.8 0.1 reduce
  0.9 0.2 convert_reduce_fusion.2
  1.1 0.1 convert_reduce_fusion
  1.3 0.8 %copy.7.slot_ids = s32[5120,1]{1,0:T(8,128)S(1)} copy(s32[5120,1]{0,1:T(1,128)S(1)} %bitcast.9) | data formatting | bytes 40960 | tf_op jit(solution)/shard_map/broadcast_in_dim | solution.py:460
  2.1 0.0 copy-start
  2.3 1.9 %fusion = f32[1024]{0:T(1024)S(1)} fusion(bf16[1024,768]{1,0:T(8,128)(2,1)} %param.2), kind=kLoop, calls=%fused_computation.2 | loop fusion | flops 2358272 | bytes 1576960 | tf_op jit(solution)/shard_map/reduce_sum | solution.py:25
  4.2 0.0 copy-done
  4.2 0.3 fusion.1.u_ref
  4.5 57.3 %shard_map.28 = f32[1,1024]{1,0:T(1,128)S(1)} custom-call(bf16[1024,768]{1,0:T(8,128)(2,1)S(1)} %fusion.1.u_ref, s32[5120,1]{1,0:T(8,128)S(1)} %copy.7.slot_ids, s32[1,1024]{1,0:T(1,128)S(1)} %compare_select_fusion.4.own_ids, s32[2,1024]{1,0:T(2,128)S(1)} %pad_add_fusion.1.res_ids, s32[2,1024]{1,0:T(2,128)S(1)} %pad_add_fusion.2.part_ids), custom_call_target="tpu_custom_call" | custom-call | tf_op jit(solution)/shard_map/pallas_call | solution.py:466
  61.8 0.6 copy.9
  (15 shorter events, 0.1 us)
Async XLA Ops:
  2.1 2.0 %copy-start = (bf16[1024,768]{1,0:T(8,128)(2,1)S(1)}, bf16[1024,768]{1,0:T(8,128)(2,1)}, u32[]{:S(2)}) copy-start(bf16[1024,768]{1,0:T(8,128)(2,1)} %param.2) | copy-start | bytes 4718596

commit v4 on v3

--- a/solution.py
+++ b/solution.py
@@ -87,7 +87,7 @@
 MESH = pl.DeviceIdType.MESH
 
 
-def kernel(line, u_ref, slot_ids, own_ids, res_ids, part_ids, out_ref,
+def kernel(line, raw_ref, ends_row, ends_column, out_ref, u_ref, slot_ids, own_ids, res_ids, part_ids,
            stream, part, row_best, res_best, part_best, own_best, message, returned, part_back, pair_back,
            out_send, swap_send, own_recv, part_send, part_recv, flow_send, ret_send, ret_recv,
            pb_send, pb_recv, pair_send, pair_recv, turn):
@@ -117,6 +117,16 @@
     def _():
         for helper in range(line):
             greet(3 - o, jnp.int32(helper))
+
+    def unit_step(c, carry):
+        at = pl.ds(pl.multiple_of(c * CHUNK, CHUNK), CHUNK)
+        u_ref[at, :] = normalize(raw_ref[at, :])
+        return carry
+
+    lax.fori_loop(0, chunks, unit_step, 0)
+
+    @pl.when(is_middle)
+    def _():
         pl.semaphore_wait(barrier, 3 * line - 1)
 
     @pl.when(is_end)
@@ -232,11 +242,31 @@
 
     own_best[...] = jnp.full_like(own_best, FLOOR)
 
+    def located(block):
+        shape = (ends_column.shape[0], rows)
+        position = block * rows + lax.broadcasted_iota(jnp.int32, shape, 1)
+        return jnp.sum(jnp.where(position >= ends_column[...], 1.0, 0.0), axis=0, keepdims=True)
+
+    def locate_rows(first, block):
+        def step(c, carry):
+            shape = (CHUNK, ends_row.shape[1])
+            position = block * rows + c * CHUNK + lax.broadcasted_iota(jnp.int32, shape, 0)
+            at = pl.ds(pl.multiple_of(first * rows + c * CHUNK, CHUNK), CHUNK)
+            slot_ids[at, :] = jnp.sum(jnp.where(position >= ends_row[...], 1.0, 0.0), axis=1, keepdims=True)
+            return carry
+
+        lax.fori_loop(0, chunks, step, 0)
+
+    def locate():
+        own_ids[...] = located(o * line + z)
+        locate_rows(line, o * line + z)
+
     @pl.when(is_outer)
     def _():
         @pl.when(is_middle)
         def _():
             each_chunk(lambda c: inward_middle(c).start())
+            locate()
             for c in range(chunks - 1):
                 inward_middle(c).wait_send()
             pl.semaphore_signal(turn, inc=1, device_id={"owner": sibling, "helper": outer}, device_id_type=MESH)
@@ -244,6 +274,7 @@
 
         @pl.when(is_end)
         def _():
+            locate()
             pl.semaphore_wait(turn, 1)
             each_chunk(lambda c: inward_end(c).start())
 
@@ -268,6 +299,16 @@
         res_best[...] = jnp.full_like(res_best, FLOOR)
         part_best[...] = jnp.full_like(part_best, FLOOR)
 
+        def locate_all():
+            locate()
+            res_ids[0:1, :] = located(held * line + near)
+            res_ids[1:2, :] = located(held * line + outer)
+            shared = (1 + jnp.minimum(o, 1)) * line
+            part_ids[0:1, :] = located(shared + near)
+            part_ids[1:2, :] = located(shared + outer)
+            for slot in range(line):
+                locate_rows(slot, held * line + slot)
+
         def kept(c):
             keep(c).wait()
 
@@ -278,7 +319,7 @@
         @pl.when(is_end)
         def _():
             each_chunk(kept)
-
+            locate_all()
             each_chunk(self_chunk)
 
         def first(c):
@@ -295,6 +336,7 @@
 
         @pl.when(is_middle)
         def _():
+            locate_all()
             each_chunk(first)
 
         @pl.when(is_end)
@@ -450,25 +492,20 @@
 
 
 def chain_body(line, embeddings, cluster_sizes):
-    unit_rows = normalize(embeddings)
-    rows, width = unit_rows.shape
+    rows, width = embeddings.shape
     ends = jnp.cumsum(cluster_sizes)
-    o, z = lax.axis_index("owner"), lax.axis_index("helper")
-    held = jnp.where((o == 1) | (o == 2), 3 - o, o)
-    ids = lambda block, total: cluster_of(block * rows, total, ends)
-    own_ids = ids(o * line + z, rows)
-    slot_ids = jnp.concatenate([ids(held * line, rows * line), own_ids])[:, None]
-    near, outer = 1 + z // 2, 3 * (z // 2)
-    shared = jnp.where(o == 0, 1, 2) * line
-    res_ids = jnp.stack([ids(held * line + near, rows), ids(held * line + outer, rows)])
-    part_ids = jnp.stack([ids(shared + near, rows), ids(shared + outer, rows)])
     chunks = rows // CHUNK
     best = pl.pallas_call(
         functools.partial(kernel, line),
         out_shape=jax.ShapeDtypeStruct((1, rows), jnp.float32),
-        in_specs=[pl.BlockSpec(memory_space=pltpu.VMEM)] * 5,
+        in_specs=[pl.BlockSpec(memory_space=pltpu.VMEM)] * 3,
         out_specs=pl.BlockSpec(memory_space=pltpu.VMEM),
         scratch_shapes=[
+            pltpu.VMEM((rows, width), jnp.bfloat16),
+            pltpu.VMEM(((line + 1) * rows, 1), jnp.float32),
+            pltpu.VMEM((1, rows), jnp.float32),
+            pltpu.VMEM((2, rows), jnp.float32),
+            pltpu.VMEM((2, rows), jnp.float32),
             pltpu.VMEM((line, rows, width), jnp.bfloat16),
             pltpu.VMEM((2, rows, width), jnp.bfloat16),
             pltpu.VMEM((line, rows, 128), jnp.float32),
@@ -496,7 +533,7 @@
         compiler_params=pltpu.CompilerParams(
             collective_id=0, has_side_effects=True, vmem_limit_bytes=48 * 2**20
         ),
-    )(unit_rows, slot_ids, own_ids[None], res_ids, part_ids)
+    )(embeddings, ends[None], ends[:, None])
     return best.reshape(rows)
 
 

time: 62.8 us -> 60.8 us (0.968)
  other arithmetic: 2.81 us -> 0.17 us
    reduce_sum x3 -> x0, other arithmetic: 2.19 us -> none  [the longest x1 1.88 us: normalize(): jnp.mean(values * values, axis=1, keepdims=True) + 1e-06]
    unnamed x3, local copies, waits for them, and re-layouts: 0.6 us -> 2 us
    broadcast_in_dim x1 -> x0, local copies, waits for them, and re-layouts: 0.78 us -> none  [chain_body(): jnp.concatenate([ids(held * line, rows * line), own_ids])[:, None]]
    another operation x1 -> x0, local copies, waits for them, and re-layouts: 0.74 us -> none
    reshape x0 -> x1, local copies, waits for them, and re-layouts: none -> 0.74 us
where the time goes in v4:
time: 60.8 us; the launch traced here: 60.3 us
  Pallas kernels  57.4 us (94%)
  local copies, waits for them, and re-layouts  2.74 us (5%)
    pallas_call x1, Pallas kernels, chain_body(): pl.pallas_call(functools.partial(kernel, line), out_shape=jax.ShapeDtypeS...  57.4 us
    unnamed x3, local copies, waits for them, and re-layouts  2 us

profile of v4, /device:TPU:1, one launch (start us, length us, event | category | flops | bytes accessed | tf_op | source)
XLA Modules:
  0.0 60.3 jit_solution(12462132306971666201)
XLA Ops:
  0.0 0.7 %copy.4 = s32[32,1]{1,0:T(8,128)S(1)} copy(s32[32,1]{0,1:T(1,128)} %bitcast.5) | data formatting | bytes 256 | tf_op jit(solution)/shard_map/reshape
  0.7 0.1 broadcast_in_dim.8.ends_column
  0.8 0.1 reduce
  0.9 0.0 copy-start
  0.9 1.4 %copy-done = bf16[1024,768]{1,0:T(8,128)(2,1)S(1)} copy-done((bf16[1024,768]{1,0:T(8,128)(2,1)S(1)}, bf16[1024,768]{1,0:T(8,128)(2,1)}, u32[]{:S(2)}) %copy-start) | copy-done | bytes 1572888
  2.3 57.4 %shard_map.28 = f32[1,1024]{1,0:T(1,128)S(1)} custom-call(bf16[1024,768]{1,0:T(8,128)(2,1)S(1)} %copy-done, s32[1,32]{1,0:T(1,128)S(1)} %bitcast.4, s32[32,1]{1,0:T(8,128)S(1)} %broadcast_in_dim.8.ends_column), custom_call_target="tpu_custom_call" | custom-call | tf_op jit(solution)/shard_map/pallas_call | solution.py:498
  59.7 0.6 copy.6
Async XLA Ops:
  0.9 1.4 %copy-start = (bf16[1024,768]{1,0:T(8,128)(2,1)S(1)}, bf16[1024,768]{1,0:T(8,128)(2,1)}, u32[]{:S(2)}) copy-start(bf16[1024,768]{1,0:T(8,128)(2,1)} %raw_ref.1) | copy-start | bytes 4718596

commit v5 on v4

--- a/solution.py
+++ b/solution.py
@@ -455,7 +455,7 @@
         pair_home.wait_recv()
         own_best[...] = jnp.maximum(own_best[...], pair_back[...])
 
-    out_ref[...] = jnp.maximum(jnp.max(own_best[...], axis=0, keepdims=True), -1.0)
+    out_ref[...] = own_best[...]
 
     @pl.when(is_outer & is_end)
     def _():
@@ -497,7 +497,7 @@
     chunks = rows // CHUNK
     best = pl.pallas_call(
         functools.partial(kernel, line),
-        out_shape=jax.ShapeDtypeStruct((1, rows), jnp.float32),
+        out_shape=jax.ShapeDtypeStruct((8, rows), jnp.float32),
         in_specs=[pl.BlockSpec(memory_space=pltpu.VMEM)] * 3,
         out_specs=pl.BlockSpec(memory_space=pltpu.VMEM),
         scratch_shapes=[
@@ -534,7 +534,7 @@
             collective_id=0, has_side_effects=True, vmem_limit_bytes=48 * 2**20
         ),
     )(embeddings, ends[None], ends[:, None])
-    return best.reshape(rows)
+    return jnp.maximum(jnp.max(best, axis=0), -1.0)
 
 
 def solution(mesh):

time: 60.8 us -> 60.8 us (level)
  other arithmetic: 0.17 us -> 0.78 us
    unnamed x3 -> x2, local copies, waits for them, and re-layouts: 2 us -> 1.41 us
where the time goes in v5:
time: 60.8 us; the launch traced here: 60.3 us
  Pallas kernels  57.4 us (94%)
  local copies, waits for them, and re-layouts  2.14 us (4%)
  other arithmetic  0.78 us (1%)
    pallas_call x1, Pallas kernels, chain_body(): pl.pallas_call(functools.partial(kernel, line), out_shape=jax.ShapeDtypeS...  57.4 us
    unnamed x2, local copies, waits for them, and re-layouts  1.41 us

profile of v5, /device:TPU:1, one launch (start us, length us, event | category | flops | bytes accessed | tf_op | source)
XLA Modules:
  0.0 60.3 jit_solution(13526251433233241509)
XLA Ops:
  0.0 0.7 %copy.4 = s32[32,1]{1,0:T(8,128)S(1)} copy(s32[32,1]{0,1:T(1,128)} %bitcast.3) | data formatting | bytes 256 | tf_op jit(solution)/shard_map/reshape
  0.7 0.1 broadcast_in_dim.8.ends_column
  0.8 0.1 reduce
  0.9 0.0 copy-start
  0.9 1.4 %copy-done = bf16[1024,768]{1,0:T(8,128)(2,1)S(1)} copy-done((bf16[1024,768]{1,0:T(8,128)(2,1)S(1)}, bf16[1024,768]{1,0:T(8,128)(2,1)}, u32[]{:S(2)}) %copy-start) | copy-done | bytes 1572888
  2.3 57.4 %shard_map.28 = f32[8,1024]{1,0:T(8,128)S(1)} custom-call(bf16[1024,768]{1,0:T(8,128)(2,1)S(1)} %copy-done, s32[1,32]{1,0:T(1,128)S(1)} %bitcast.2, s32[32,1]{1,0:T(8,128)S(1)} %broadcast_in_dim.8.ends_column), custom_call_target="tpu_custom_call" | custom-call | tf_op jit(solution)/shard_map/pallas_call | solution.py:498
  59.7 0.6 broadcast_maximum_fusion
  (1 shorter events, 0.0 us)
Async XLA Ops:
  0.9 1.4 %copy-start = (bf16[1024,768]{1,0:T(8,128)(2,1)S(1)}, bf16[1024,768]{1,0:T(8,128)(2,1)}, u32[]{:S(2)}) copy-start(bf16[1024,768]{1,0:T(8,128)(2,1)} %raw_ref.1) | copy-start | bytes 4718596
